TPU v7x, 32 devices: a whole 2x2x4 slice. The times are simulated.
32 devices in a mesh: groups: 2 (over x), row: 8 (over z, y), col: 2 (over core).
Axes of the slice: x: 2, y: 2, z: 4, core: 2. Of those that a mesh axis runs over, the one named last changes fastest.
Arguments:
- right_side: float32 [32, 4096], P('groups', ('row', 'col')), parts along dimension 0, may hold values from -6 to 6
- current_ratio: float32 [8192], P(('groups', 'row', 'col')), parts along dimension 0, may hold values from 0.7 to 1
- filament_xy: float32 [2, 6400], replicated, may hold values from -0.3 to 0.3
- element_offset: float32 [2, 8192], P(None, 'groups'), parts along dimension 1, may hold values from -0.003 to 0.003
- element_filament: int32 [8192], P('groups'), parts along dimension 0, may hold values from 0 to 6399
- element_order: int32 [8192], P('groups'), parts along dimension 0, may hold values from 0 to 4095, each once
Outputs:
- solution: float32 [32, 4096], P('groups', ('row', 'col')), parts along dimension 0
- residual: float32 [32, 4096], P('groups', ('row', 'col')), parts along dimension 0
There are 2 independent parts, one for each index of `groups`. A program takes and returns all parts, laid end to end along the dimension named above; an argument that names none is the same for every part. Nothing has to cross between parts.
Inputs may be any that keep to these rules, and one draw needn't show every extreme that they name: `element_order`: each position appears once.
All inputs are finite; a program needn't handle non-finite values.
Results may differ from a plain program's by a relative error of at most 0.00014.
Values sent between devices are 32-bit elements; how exact they have to be, the bound alone decides.
A program may use at most 128 MiB of HBM per device.

v0:
```python
import math
import jax
import jax.numpy as jnp
from jax import lax
from jax.sharding import PartitionSpec as P

ITERS = 2
EPS_SQUARED = 0.0001
COUPLE = 0.3


def kernel(left_x, left_y, right_x, right_y):
    delta_x = left_x[:, None] - right_x[None, :]
    delta_y = left_y[:, None] - right_y[None, :]
    return lax.rsqrt(delta_x * delta_x + delta_y * delta_y + EPS_SQUARED)


def on_device(
    right_side, current_ratio, filament_xy, element_offset, element_filament, element_order
):
    row_devices = lax.axis_size("row")
    col_devices = lax.axis_size("col")
    side_count = right_side.shape[0]
    local_count = right_side.shape[1]
    element_count = local_count * row_devices * col_devices
    coupling_scale = COUPLE / math.sqrt(element_count)
    places = filament_xy[:, element_filament[element_order]] + element_offset[:, element_order]
    diagonal = 1.0 + 8.0 * current_ratio**24
    row_index = lax.axis_index("row")
    col_index = lax.axis_index("col")
    col_width = local_count * col_devices
    col_xy = lax.dynamic_slice_in_dim(places, row_index * col_width, col_width, 1)
    row_xy = lax.dynamic_index_in_dim(
        places.reshape(2, row_devices, col_devices, local_count), col_index, 2, False
    )
    solution = jnp.zeros_like(right_side)
    residual = right_side
    direction = right_side

    def squares(vector):
        return lax.psum(jnp.sum(vector * vector, axis=1, keepdims=True), ("row", "col"))

    norm_now = squares(residual)
    for iteration in range(ITERS):
        wide = lax.all_gather(direction, "col", axis=1, tiled=True)
        peer_count = side_count * lax.axis_size("row") // side_count
        group_size = math.gcd(peer_count, 8)
        blocks = peer_count // group_size
        block_places = row_xy.reshape(2, blocks, group_size * local_count).transpose(1, 0, 2)

        def apply_block(block_xy):
            coupling = kernel(col_xy[0], col_xy[1], block_xy[0], block_xy[1])
            return jnp.dot(
                wide, coupling, precision=lax.Precision.HIGHEST, preferred_element_type=jnp.float32
            )

        parts = lax.map(apply_block, block_places)
        parts = parts.reshape(blocks, side_count, group_size, local_count).transpose(0, 2, 1, 3)
        summed = lax.psum_scatter(
            parts.reshape(peer_count * side_count, local_count),
            "row",
            scatter_dimension=0,
            tiled=True,
        )
        image_vec = diagonal * direction + coupling_scale * summed
        curved = lax.psum(jnp.sum(direction * image_vec, axis=1, keepdims=True), ("row", "col"))
        step_length = norm_now / curved
        solution = solution + step_length * direction
        residual = residual - step_length * image_vec
        norm_next = squares(residual)
        direction = residual + norm_next / norm_now * direction
        norm_now = norm_next
    return (solution, residual)


def solution(mesh):
    return jax.shard_map(
        on_device,
        mesh=mesh,
        in_specs=(
            P("groups", ("row", "col")),
            P(("groups", "row", "col")),
            P(),
            P(None, "groups"),
            P("groups"),
            P("groups"),
        ),
        out_specs=(P("groups", ("row", "col")), P("groups", ("row", "col"))),
        check_vma=False,
    )
```

profile of v0, /device:TPU:0, one launch (start us, length us, event | category | flops | bytes accessed | tf_op | source)
XLA Modules:
  0.0 302.2 jit_solution(8599823185604984722)
XLA Ops:
  7.2 0.0 copy-start
  7.2 0.0 reduce-scatter.3.cloned.1.call-start
  7.2 0.7 fusion.12
  8.0 0.0 copy-done
  8.0 23.0 %gather_fusion = s32[4096]{0:T(1024)S(1)} fusion(s32[4096]{0:T(1024)S(1)} %copy-done, s32[4096]{0:T(1024)S(1)} %fusion.12), kind=kCustom, calls=%fused_computation | custom fusion | bytes 49152 | tf_op jit(solution)/shard_map/gather | solution.py:27
  31.0 0.0 copy-start.4
  31.1 1.1 copy.12
  32.2 2.0 copy.13
  34.1 15.7 %gather_fusion.2 = f32[4096,2]{1,0:T(8,128)} fusion(f32[2,4096]{0,1:T(8,128)} %copy.13, s32[4096]{0:T(1024)S(1)} %fusion.12), kind=kCustom, calls=%fused_computation.2 | custom fusion | bytes 81920 | tf_op jit(solution)/shard_map/gather | solution.py:27
  49.8 14.1 %gather_fusion.1 = f32[4096,2]{1,0:T(8,128)} fusion(f32[2,6400]{0,1:T(8,128)S(1)} %copy.12, s32[4096]{0:T(1024)S(1)} %broadcast_clamp_fusion), kind=kCustom, calls=%fused_computation.1 | custom fusion | bytes 81920 | tf_op jit(solution)/shard_map/gather | solution.py:27
  63.9 2.4 add.92
  66.4 0.3 slice_reduce_fusion.1
  66.7 0.9 dynamic-slice_reduce_fusion.1
  67.6 1.9 all_gather.6
  69.6 3.2 %fusion.1 = f32[2048,16]{0,1:T(8,128)S(1)} fusion(f32[16,512]{1,0:T(8,128)S(1)} %all_gather.6, f32[2048]{0:T(1024)S(1)} %bitcast.53, f32[512]{0:T(512)S(1)} %get-tuple-element.30, f32[2048]{0:T(1024)S(1)} %bitcast.51, f32[512]{0:T(512)S(1)} %get-tuple-element.24), kind=kOutput, calls=%fused_computation.5 | convolution fusion | flops 207618048 | bytes 184320 | tf_op jit(solution)/shard_map/while/body/eval_jaxpr/dot_general | solution.py:53
  72.9 0.7 copy.15
  73.6 0.0 reduce-scatter.3.cloned.1.call-update
  73.6 0.0 reduce-scatter.5.cloned.1.call-start
  73.7 63.9 %reduce-scatter.3.cloned.1.call-done = f32[16,256]{1,0:T(8,128)} async-done(((f32[128,256]{1,0:T(8,128)}), f32[16,256]{1,0:T(8,128)}) %reduce-scatter.3.cloned.1.call-update) | async-done | bytes 16400 | tf_op jit(solution)/shard_map/reduce_scatter | solution.py:59
  137.6 0.8 multiply_reduce_fusion.2
  138.4 29.7 %all-reduce = (f32[16,1]{0,1:T(1,128)S(1)}, f32[16,1]{0,1:T(1,128)S(1)}) all-reduce(f32[16,1]{0,1:T(1,128)S(1)} %bitcast.56, f32[16,1]{0,1:T(1,128)S(1)} %bitcast.55), channel_id=1, replica_groups=mesh['groups'=2,'row'=8,'col'=2] {'row','col'}, use_global_device_ids=true, to_apply=%region_1.2 | all-reduce | flops 32 | bytes 256 | tf_op jit(solution)/shard_map/psum | solution.py:41
  168.1 0.9 multiply_reduce_fusion.1
  169.0 29.5 %psum.30 = f32[16,1]{0,1:T(1,128)S(1)} all-reduce(f32[16,1]{0,1:T(1,128)S(1)} %bitcast.57), channel_id=1, replica_groups=mesh['groups'=2,'row'=8,'col'=2] {'row','col'}, use_global_device_ids=true, to_apply=%region_6.7 | all-reduce | flops 16 | bytes 128 | tf_op jit(solution)/shard_map/psum | solution.py:41
  198.5 0.8 multiply_add_fusion.2
  199.3 1.8 all_gather.7
  201.1 3.1 %fusion = f32[16,2048]{1,0:T(8,128)S(1)} fusion(f32[16,512]{1,0:T(8,128)S(1)} %all_gather.7, f32[2048]{0:T(1024)S(1)} %bitcast.54, f32[512]{0:T(512)S(1)} %get-tuple-element.30, f32[2048]{0:T(1024)S(1)} %bitcast.52, f32[512]{0:T(512)S(1)} %get-tuple-element.24), kind=kOutput, calls=%fused_computation.4 | convolution fusion | flops 207618048 | bytes 184320 | tf_op jit(solution)/shard_map/while/body/eval_jaxpr/dot_general | solution.py:53
  204.2 0.7 copy.16
  204.9 0.0 reduce-scatter.5.cloned.1.call-update
  204.9 58.5 %reduce-scatter.5.cloned.1.call-done = f32[16,256]{1,0:T(8,128)} async-done(((f32[128,256]{1,0:T(8,128)}), f32[16,256]{1,0:T(8,128)}) %reduce-scatter.5.cloned.1.call-update) | async-done | bytes 16400 | tf_op jit(solution)/shard_map/reduce_scatter | solution.py:59
  263.4 0.8 multiply_reduce_fusion
  264.3 29.6 %psum.31 = f32[16,1]{0,1:T(1,128)S(1)} all-reduce(f32[16,1]{0,1:T(1,128)S(1)} %bitcast.58), channel_id=1, replica_groups=mesh['groups'=2,'row'=8,'col'=2] {'row','col'}, use_global_device_ids=true, to_apply=%region_9.10 | all-reduce | flops 16 | bytes 128 | tf_op jit(solution)/shard_map/psum | solution.py:66
  293.9 1.4 multiply_subtract_fusion
  (22 shorter events, 0.2 us)
Async XLA Ops:
  7.2 0.8 copy-start
  7.2 130.4 %reduce-scatter.3.cloned.1.call-start = ((), (), s32[]{:S(2)}) async-start(), calls=%async_computation.2 | async-start | bytes 147456 | tf_op jit(solution)/shard_map/reduce_scatter | solution.py:59
  8.0 23.1 %copy-start.3 = (f32[2,6400]{1,0:T(2,128)S(1)}, f32[2,6400]{1,0:T(2,128)}, u32[]{:S(2)}) copy-start(f32[2,6400]{1,0:T(2,128)} %param.8) | copy-start | bytes 153604
  31.0 1.2 copy-start.4
  63.9 3.7 %copy-start.1 = (f32[16,256]{1,0:T(8,128)S(1)}, f32[16,256]{1,0:T(8,128)}, u32[]{:S(2)}) copy-start(f32[16,256]{1,0:T(8,128)} %param.6) | copy-start | bytes 49156
  69.6 4.1 %copy-start.5 = (f32[256]{0:T(256)S(1)}, f32[256]{0:T(256)}, u32[]{:S(2)}) copy-start(f32[256]{0:T(256)} %param.7) | copy-start | bytes 3076
  73.6 189.9 %reduce-scatter.5.cloned.1.call-start = ((), (), s32[]{:S(2)}) async-start(), calls=%async_computation.3 | async-start | bytes 147456 | tf_op jit(solution)/shard_map/reduce_scatter | solution.py:59
  201.1 92.9 %copy-start.2 = (f32[16,256]{1,0:T(8,128)S(1)}, f32[16,256]{1,0:T(8,128)}, u32[]{:S(2)}) copy-start(f32[16,256]{1,0:T(8,128)} %reduce-scatter.3.cloned.1.call-done) | copy-start | bytes 49156
Sparse Core Ops, SparseCore 0:
  73.7 63.8 reduce-scatter.2
  205.0 58.3 reduce-scatter.4
where the time goes:
time: 303 us; the launch traced here: 302 us
  waiting for transfers between devices  122 us (40%)
  blocking collectives  92.5 us (31%)
  local copies, waits for them, and re-layouts  58.6 us (19%)
  between operations  14.2 us (5%)
  other arithmetic  8 us (3%)
  matrix products  6.3 us (2%)
    reduce_scatter x2, waiting for transfers between devices, on_device(): lax.psum_scatter(parts.reshape(peer_count * side_count, local_count), 'ro...  122 us
    psum x2, blocking collectives, squares(): lax.psum(jnp.sum(vector * vector, axis=1, keepdims=True), ('row', 'col'))  59.1 us
    psum x1, blocking collectives, on_device(): lax.psum(jnp.sum(direction * image_vec, axis=1, keepdims=True), ('row', '...  29.6 us
    gather x1, local copies, waits for them, and re-layouts, on_device(): element_filament[element_order]  23 us
    gather x1, local copies, waits for them, and re-layouts, on_device(): element_offset[:, element_order]  15.7 us
    gather x1, local copies, waits for them, and re-layouts, on_device(): filament_xy[:, element_filament[element_order]]  14.1 us
    dot_general x2, matrix products, apply_block(): jnp.dot(wide, coupling, precision=lax.Precision.HIGHEST, preferred_elemen...  6.3 us
  transfers between devices with their start and end apart: 2, of which 2 were waited for; matrix products, arithmetic and copies ran while one was open for 0% of the time, Pallas kernels for 0%

commit v1 on v0

--- a/solution.py
+++ b/solution.py
@@ -7,6 +7,11 @@
 ITERS = 2
 EPS_SQUARED = 0.0001
 COUPLE = 0.3
+
+
+def _manage_modes(field, shard_axis, across="row"):
+    step_out = lax.psum(field, axis_name=shard_axis)
+    return lax.psum(step_out, across)
 
 
 def kernel(left_x, left_y, right_x, right_y):
@@ -63,7 +68,7 @@
             tiled=True,
         )
         image_vec = diagonal * direction + coupling_scale * summed
-        curved = lax.psum(jnp.sum(direction * image_vec, axis=1, keepdims=True), ("row", "col"))
+        curved = _manage_modes(jnp.sum(direction * image_vec, axis=1, keepdims=True), "col")
         step_length = norm_now / curved
         solution = solution + step_length * direction
         residual = residual - step_length * image_vec

time: 303 us -> 317 us (1.046)
  blocking collectives: 92.5 us -> 106 us
    psum x1 -> x4, blocking collectives: 29.6 us -> 41.5 us  [the longest x2 36.5 us: _manage_modes(): return lax.psum(step_out, across)]
where the time goes in v1:
time: 317 us; the launch traced here: 316 us
  waiting for transfers between devices  123 us (39%)
  blocking collectives  106 us (33%)
  local copies, waits for them, and re-layouts  58.6 us (18%)
  between operations  14.2 us (4%)
  other arithmetic  8 us (3%)
  matrix products  6.3 us (2%)
    reduce_scatter x2, waiting for transfers between devices, on_device(): lax.psum_scatter(parts.reshape(peer_count * side_count, local_count), 'ro...  123 us
    psum x2, blocking collectives, squares(): lax.psum(jnp.sum(vector * vector, axis=1, keepdims=True), ('row', 'col'))  61 us
    psum x2, blocking collectives, _manage_modes(): return lax.psum(step_out, across)  36.5 us
    gather x1, local copies, waits for them, and re-layouts, on_device(): element_filament[element_order]  23 us
    gather x1, local copies, waits for them, and re-layouts, on_device(): element_offset[:, element_order]  15.7 us
    gather x1, local copies, waits for them, and re-layouts, on_device(): filament_xy[:, element_filament[element_order]]  14.1 us
  transfers between devices with their start and end apart: 2, of which 2 were waited for; matrix products, arithmetic and copies ran while one was open for 0% of the time, Pallas kernels for 0%

profile of v1, /device:TPU:0, one launch (start us, length us, event | category | flops | bytes accessed | tf_op | source)
XLA Modules:
  0.0 316.1 jit_solution(6051255472083876375)
XLA Ops:
  7.2 0.0 reduce-scatter.3.cloned.1.call-start
  7.2 0.7 fusion.12
  8.0 23.0 %gather_fusion = s32[4096]{0:T(1024)S(1)} fusion(s32[4096]{0:T(1024)S(1)} %copy-done, s32[4096]{0:T(1024)S(1)} %fusion.12), kind=kCustom, calls=%fused_computation | custom fusion | bytes 49152 | tf_op jit(solution)/shard_map/gather | solution.py:32
  31.1 1.1 copy.12
  32.2 2.0 copy.13
  34.1 15.7 %gather_fusion.2 = f32[4096,2]{1,0:T(8,128)} fusion(f32[2,4096]{0,1:T(8,128)} %copy.13, s32[4096]{0:T(1024)S(1)} %fusion.12), kind=kCustom, calls=%fused_computation.2 | custom fusion | bytes 81920 | tf_op jit(solution)/shard_map/gather | solution.py:32
  49.8 14.1 %gather_fusion.1 = f32[4096,2]{1,0:T(8,128)} fusion(f32[2,6400]{0,1:T(8,128)S(1)} %copy.12, s32[4096]{0:T(1024)S(1)} %broadcast_clamp_fusion), kind=kCustom, calls=%fused_computation.1 | custom fusion | bytes 81920 | tf_op jit(solution)/shard_map/gather | solution.py:32
  63.9 2.4 add.96
  66.4 0.3 slice_reduce_fusion.1
  66.7 0.9 dynamic-slice_reduce_fusion.1
  67.6 1.9 all_gather.6
  69.6 3.2 %fusion.1 = f32[2048,16]{0,1:T(8,128)S(1)} fusion(f32[16,512]{1,0:T(8,128)S(1)} %all_gather.6, f32[2048]{0:T(1024)S(1)} %bitcast.53, f32[512]{0:T(512)S(1)} %get-tuple-element.30, f32[2048]{0:T(1024)S(1)} %bitcast.51, f32[512]{0:T(512)S(1)} %get-tuple-element.24), kind=kOutput, calls=%fused_computation.5 | convolution fusion | flops 207618048 | bytes 184320 | tf_op jit(solution)/shard_map/while/body/eval_jaxpr/dot_general | solution.py:58
  72.9 0.7 copy.15
  73.6 0.0 reduce-scatter.3.cloned.1.call-update
  73.6 0.0 reduce-scatter.5.cloned.1.call-start
  73.7 63.9 %reduce-scatter.3.cloned.1.call-done = f32[16,256]{1,0:T(8,128)} async-done(((f32[128,256]{1,0:T(8,128)}), f32[16,256]{1,0:T(8,128)}) %reduce-scatter.3.cloned.1.call-update) | async-done | bytes 16400 | tf_op jit(solution)/shard_map/reduce_scatter | solution.py:64
  137.6 0.8 multiply_reduce_fusion.2
  138.4 2.5 psum.43
  140.9 31.6 %psum.42 = f32[16,1]{0,1:T(1,128)S(1)} all-reduce(f32[16,1]{0,1:T(1,128)S(1)} %bitcast.55), channel_id=1, replica_groups=mesh['groups'=2,'row'=8,'col'=2] {'row','col'}, use_global_device_ids=true, to_apply=%region_1.2 | all-reduce | flops 16 | bytes 128 | tf_op jit(solution)/shard_map/psum | solution.py:46
  172.4 17.1 %psum.44 = f32[16,1]{0,1:T(1,128)S(1)} all-reduce(f32[16,1]{0,1:T(1,128)S(1)} %psum.43), channel_id=1, replica_groups=mesh['groups'=2,'row'=8,'col'=2] {'row'}, use_global_device_ids=true, to_apply=%region_5.6 | all-reduce | flops 16 | bytes 128 | tf_op jit(solution)/shard_map/psum | solution.py:14
  189.6 0.9 multiply_reduce_fusion.1
  190.5 29.5 %psum.45 = f32[16,1]{0,1:T(1,128)S(1)} all-reduce(f32[16,1]{0,1:T(1,128)S(1)} %bitcast.57), channel_id=1, replica_groups=mesh['groups'=2,'row'=8,'col'=2] {'row','col'}, use_global_device_ids=true, to_apply=%region_7.8 | all-reduce | flops 16 | bytes 128 | tf_op jit(solution)/shard_map/psum | solution.py:46
  220.0 0.8 multiply_add_fusion.2
  220.7 1.8 all_gather.7
  222.6 3.1 fusion
  225.7 0.7 copy.16
  226.4 0.0 reduce-scatter.5.cloned.1.call-update
  226.4 58.7 %reduce-scatter.5.cloned.1.call-done = f32[16,256]{1,0:T(8,128)} async-done(((f32[128,256]{1,0:T(8,128)}), f32[16,256]{1,0:T(8,128)}) %reduce-scatter.5.cloned.1.call-update) | async-done | bytes 16400 | tf_op jit(solution)/shard_map/reduce_scatter | solution.py:64
  285.1 0.8 multiply_reduce_fusion
  285.9 2.5 psum.46
  288.4 19.4 %psum.47 = f32[16,1]{0,1:T(1,128)S(1)} all-reduce(f32[16,1]{0,1:T(1,128)S(1)} %psum.46), channel_id=1, replica_groups=mesh['groups'=2,'row'=8,'col'=2] {'row'}, use_global_device_ids=true, to_apply=%region_11.12 | all-reduce | flops 16 | bytes 128 | tf_op jit(solution)/shard_map/psum | solution.py:14
  307.8 1.4 multiply_subtract_fusion
  (25 shorter events, 0.2 us)
Async XLA Ops:
  7.2 0.8 copy-start
  7.2 130.4 %reduce-scatter.3.cloned.1.call-start = ((), (), s32[]{:S(2)}) async-start(), calls=%async_computation.2 | async-start | bytes 147456 | tf_op jit(solution)/shard_map/reduce_scatter | solution.py:64
  8.0 23.1 %copy-start.3 = (f32[2,6400]{1,0:T(2,128)S(1)}, f32[2,6400]{1,0:T(2,128)}, u32[]{:S(2)}) copy-start(f32[2,6400]{1,0:T(2,128)} %param.8) | copy-start | bytes 153604
  31.0 1.2 copy-start.4
  63.9 3.7 %copy-start.1 = (f32[16,256]{1,0:T(8,128)S(1)}, f32[16,256]{1,0:T(8,128)}, u32[]{:S(2)}) copy-start(f32[16,256]{1,0:T(8,128)} %param.6) | copy-start | bytes 49156
  69.6 4.1 %copy-start.5 = (f32[256]{0:T(256)S(1)}, f32[256]{0:T(256)}, u32[]{:S(2)}) copy-start(f32[256]{0:T(256)} %param.7) | copy-start | bytes 3076
  73.6 211.5 %reduce-scatter.5.cloned.1.call-start = ((), (), s32[]{:S(2)}) async-start(), calls=%async_computation.3 | async-start | bytes 147456 | tf_op jit(solution)/shard_map/reduce_scatter | solution.py:64
  222.6 85.2 %copy-start.2 = (f32[16,256]{1,0:T(8,128)S(1)}, f32[16,256]{1,0:T(8,128)}, u32[]{:S(2)}) copy-start(f32[16,256]{1,0:T(8,128)} %reduce-scatter.3.cloned.1.call-done) | copy-start | bytes 49156
Sparse Core Ops, SparseCore 0:
  73.7 63.8 reduce-scatter.2
  226.5 58.4 reduce-scatter.4
